TPU v7x, 256 devices: a whole 4x4x8 slice. The times are simulated.
256 devices in a mesh: dp: 8 (over z), expert: 32 (over x, y, core).
Axes of the slice: x: 4, y: 4, z: 8, core: 2. Of those that a mesh axis runs over, the one named last changes fastest.
Arguments:
- tokens: bfloat16 [2048, 7168], P('expert', 'dp'), may hold values from -6 to 6
- tangent: bfloat16 [2048, 7168], P('expert', 'dp'), may hold values from -6 to 6
- cotangent: bfloat16 [2048, 7168], P('expert', 'dp'), may hold values from -3 to 3
- routing: int32 [2048, 8], P('expert'), may hold values from 0 to 31, all different within a row; in each aligned block of 64 rows (0 to 63, 64 to 127, ...) at most 18 rows name the same one
- gate_weights: float32 [2048, 8], P('expert'), may hold values from 0.1 to 0.6
- gate_proj: bfloat16 [32, 7168, 2048], P('expert', 'dp'), may hold values from -0.0625 to 0.0625
- up_proj: bfloat16 [32, 7168, 2048], P('expert', 'dp'), may hold values from -0.0625 to 0.0625
- down_proj: bfloat16 [32, 2048, 7168], P('expert', None, 'dp'), may hold values from -0.125 to 0.125
Outputs:
- hessian_product: float32 [2048, 7168], P('expert', 'dp')
Inputs may be any that keep to these rules, and one draw needn't show every extreme that they name: `routing`: each token names 8 different experts. In each aligned block of 64 tokens (the tokens of one index of expert) no expert is named more than 18 times, a bound that some block reaches.
All inputs are finite; a program needn't handle non-finite values.
Results may differ from a plain program's by a relative error of at most 0.0041.
Values may be sent and summed in bfloat16 or wider, within the bound.
A program may use at most 128 MiB of HBM per device.

v0:
```python
import jax
import jax.numpy as jnp
from jax import lax
from jax.sharding import PartitionSpec as P

TOP = 8


def second_order(pre_gate, pre_up, tangent_gate, tangent_up, back_hidden):
    sigma = jax.nn.sigmoid(pre_gate)
    first_slope = sigma * (1.0 + pre_gate * (1.0 - sigma))
    second_slope = sigma * (1.0 - sigma) * (2.0 + pre_gate * (1.0 - 2.0 * sigma))
    factor_a = back_hidden * (second_slope * tangent_gate * pre_up + first_slope * tangent_up)
    factor_b = back_hidden * first_slope * tangent_gate
    return (factor_a.astype(jnp.bfloat16), factor_b.astype(jnp.bfloat16))


def contract_last(left_rows, right_matrix):
    return lax.dot_general(
        left_rows, right_matrix, (((1,), (1,)), ((), ())), preferred_element_type=jnp.float32
    )


def shards(tokens, tangent, cotangent, routing, gate_weights, gate_proj, up_proj, down_proj):
    expert_count = lax.axis_size("expert")
    tok_rows = tokens.shape[0]
    feat_cols = tokens.shape[1]
    capacity = min(tok_rows, tok_rows * TOP // expert_count * 9 // 8)
    slot_total = expert_count * capacity
    routed_flat = routing.reshape(-1)
    route_hits = (
        routed_flat[:, None] == jnp.arange(expert_count, dtype=jnp.int32)[None, :]
    ).astype(jnp.int32)
    slot_index = jnp.sum((jnp.cumsum(route_hits, axis=0) - route_hits) * route_hits, axis=1)
    target_row = routed_flat * capacity + slot_index

    def scatter_rows(values):
        spread = jnp.repeat(values, TOP, axis=0)
        zero_buf = jnp.zeros((slot_total, values.shape[1]), values.dtype)
        return zero_buf.at[target_row].set(spread).reshape(expert_count, capacity, values.shape[1])

    x_rows = lax.all_to_all(
        scatter_rows(tokens), "expert", split_axis=0, concat_axis=0, tiled=True
    ).reshape(slot_total, feat_cols)
    paired = jnp.concatenate([tangent, cotangent], axis=1)
    paired_rows = lax.all_to_all(
        scatter_rows(paired), "expert", split_axis=0, concat_axis=0, tiled=True
    ).reshape(slot_total, 2 * feat_cols)
    v_rows = paired_rows[:, :feat_cols]
    c_rows = paired_rows[:, feat_cols:]
    gate_cols = gate_proj[0]
    up_cols = up_proj[0]
    down_rows = down_proj[0]
    part_gate = jnp.dot(x_rows, gate_cols, preferred_element_type=jnp.float32)
    part_up = jnp.dot(x_rows, up_cols, preferred_element_type=jnp.float32)
    part_tgate = jnp.dot(v_rows, gate_cols, preferred_element_type=jnp.float32)
    part_tup = jnp.dot(v_rows, up_cols, preferred_element_type=jnp.float32)
    part_back = contract_last(c_rows, down_rows)
    summed = (
        lax.psum_scatter(part_gate, "dp", scatter_dimension=0, tiled=True),
        lax.psum_scatter(part_up, "dp", scatter_dimension=0, tiled=True),
        lax.psum_scatter(part_tgate, "dp", scatter_dimension=0, tiled=True),
        lax.psum_scatter(part_tup, "dp", scatter_dimension=0, tiled=True),
        lax.psum_scatter(part_back, "dp", scatter_dimension=0, tiled=True),
    )
    factor_a, factor_b = second_order(summed[0], summed[1], summed[2], summed[3], summed[4])
    factors = jnp.stack([factor_a, factor_b])
    piece = lax.all_gather(factors, "dp", axis=1, tiled=True)
    result_rows = contract_last(piece[0], gate_cols) + contract_last(piece[1], up_cols)
    outgoing = result_rows.astype(jnp.bfloat16).reshape(expert_count, capacity, feat_cols)
    returned = lax.all_to_all(outgoing, "expert", split_axis=0, concat_axis=0, tiled=True).reshape(
        slot_total, feat_cols
    )
    gathered = returned[target_row].reshape(tok_rows, TOP, feat_cols).astype(jnp.float32)
    return jnp.sum(gate_weights[:, :, None] * gathered, axis=1)


def solution(mesh):
    in_specs = (
        P("expert", "dp"),
        P("expert", "dp"),
        P("expert", "dp"),
        P("expert", None),
        P("expert", None),
        P("expert", "dp", None),
        P("expert", "dp", None),
        P("expert", None, "dp"),
    )
    out_specs = P("expert", "dp")
    return jax.shard_map(shards, mesh=mesh, in_specs=in_specs, out_specs=out_specs, check_vma=False)
```

profile of v0, /device:TPU:1, one launch (start us, length us, event | category | flops | bytes accessed | tf_op | source)
XLA Modules:
  0.0 463.8 jit_solution(245255507557251218)
XLA Ops:
  6.5 0.8 copy.12
  7.3 0.1 eq.29
  7.4 0.1 eq.25
  7.5 0.7 broadcast_multiply_fusion
  8.2 1.2 reduce-window.6
  9.4 0.2 slice_reduce_fusion
  9.7 0.1 copy.11
  9.7 0.1 mul.66
  9.8 0.1 fusion.40
  10.0 3.0 scatter_custom_fusion.1
  12.9 0.3 reshape.79
  13.3 29.3 %all_to_all.15 = bf16[32,18,896]{2,1,0:T(8,128)(2,1)S(1)} all-to-all(bf16[32,18,896]{2,1,0:T(8,128)(2,1)S(1)} %reshape.79), channel_id=1, replica_groups=mesh['dp'=8,'expert'=32] {'expert'}, dimensions={0} | all-to-all | bytes 2064384 | tf_op jit(solution)/shard_map/all_to_all | solution.py:42
  42.6 0.3 reshape.80
  42.9 6.3 %fusion.4 = f32[576,2048]{1,0:T(8,128)} fusion(bf16[576,896]{1,0:T(8,128)(2,1)S(1)} %reshape.80, bf16[1,896,2048]{2,1,0:T(8,128)(2,1)} %param.14), kind=kOutput, calls=%fused_computation.7 | convolution fusion | flops 2113929216 | bytes 9420800 | tf_op jit(solution)/shard_map/dot_general | solution.py:55
  49.2 0.0 reduce-scatter.12.cloned.1.call-update
  49.2 0.0 reduce-scatter.8.cloned.1.call-start
  49.3 6.3 %fusion.10 = f32[576,2048]{1,0:T(8,128)} fusion(bf16[576,896]{1,0:T(8,128)(2,1)S(1)} %reshape.80, bf16[1,896,2048]{2,1,0:T(8,128)(2,1)} %param.13), kind=kOutput, calls=%fused_computation.13 | convolution fusion | flops 2113929216 | bytes 9420800 | tf_op jit(solution)/shard_map/dot_general | solution.py:54
  55.6 0.0 reduce-scatter.10.cloned.1.call-start
  55.7 0.8 copy-done.1
  56.5 0.1 copy-done.2
  56.6 4.8 %scatter_custom_fusion = bf16[576,1792]{1,0:T(8,128)(2,1)} fusion(s32[512]{0:T(512)S(1)} %bitcast.64, bf16[]{:T(256)} %constant.7.clone.1, bf16[64,1792]{1,0:T(8,128)(2,1)S(1)} %pad_maximum_fusion.1), kind=kCustom, calls=%fused_computation.22 | custom fusion | bytes 2293762 | tf_op jit(solution)/shard_map/scatter | solution.py:40
  61.4 2.6 reshape.76
  64.0 39.1 %all_to_all.16 = bf16[32,18,1792]{2,1,0:T(8,128)(2,1)} all-to-all(bf16[32,18,1792]{2,1,0:T(8,128)(2,1)S(1)} %reshape.76), channel_id=1, replica_groups=mesh['dp'=8,'expert'=32] {'expert'}, dimensions={0} | all-to-all | bytes 4128768 | tf_op jit(solution)/shard_map/all_to_all | solution.py:46
  103.1 2.8 reshape.77
  105.9 6.4 %fusion.8 = f32[576,2048]{1,0:T(8,128)} fusion(bf16[1,896,2048]{2,1,0:T(8,128)(2,1)} %param.13, bf16[576,1792]{1,0:T(8,128)(2,1)S(1)} %reshape.77), kind=kOutput, calls=%fused_computation.11 | convolution fusion | flops 2113929216 | bytes 9420800 | tf_op jit(solution)/shard_map/dot_general | solution.py:56
  112.3 0.0 reduce-scatter.10.cloned.1.call-update
  112.3 0.2 reduce-scatter.14.cloned.1.call-start
  112.6 6.3 %fusion.2 = f32[576,2048]{1,0:T(8,128)} fusion(bf16[1,896,2048]{2,1,0:T(8,128)(2,1)} %param.14, bf16[576,1792]{1,0:T(8,128)(2,1)S(1)} %reshape.77), kind=kOutput, calls=%fused_computation.5 | convolution fusion | flops 2113929216 | bytes 9420800 | tf_op jit(solution)/shard_map/dot_general | solution.py:57
  118.9 0.0 reduce-scatter.6.cloned.1.call-start
  118.9 6.4 %fusion.12 = f32[576,2048]{1,0:T(8,128)} fusion(bf16[1,2048,896]{2,1,0:T(8,128)(2,1)} %param.15, bf16[576,1792]{1,0:T(8,128)(2,1)S(1)} %reshape.77), kind=kOutput, calls=%fused_computation.15 | convolution fusion | flops 2113929216 | bytes 9420800 | tf_op jit(solution)/shard_map/dot_general | solution.py:19
  125.3 0.0 all-gather.2.cloned.1.call-start
  125.4 0.0 reduce-scatter.12.cloned.1.call-done
  125.4 44.6 %reduce-scatter.8.cloned.1.call-done = f32[72,2048]{1,0:T(8,128)} async-done(((f32[576,2048]{1,0:T(8,128)}), f32[72,2048]{1,0:T(8,128)}) %reduce-scatter.8.cloned.1.call-update) | async-done | bytes 589840 | tf_op jit(solution)/shard_map/reduce_scatter | solution.py:60
  170.0 61.5 %reduce-scatter.10.cloned.1.call-done = f32[72,2048]{1,0:T(8,128)} async-done(((f32[576,2048]{1,0:T(8,128)}), f32[72,2048]{1,0:T(8,128)}) %reduce-scatter.10.cloned.1.call-update) | async-done | bytes 589840 | tf_op jit(solution)/shard_map/reduce_scatter | solution.py:62
  231.5 61.3 %reduce-scatter.14.cloned.1.call-done = f32[72,2048]{1,0:T(8,128)} async-done(((f32[576,2048]{1,0:T(8,128)}), f32[72,2048]{1,0:T(8,128)}) %reduce-scatter.14.cloned.1.call-update) | async-done | bytes 589840 | tf_op jit(solution)/shard_map/reduce_scatter | solution.py:63
  292.8 61.3 %reduce-scatter.6.cloned.1.call-done = f32[72,2048]{1,0:T(8,128)} async-done(((f32[576,2048]{1,0:T(8,128)}), f32[72,2048]{1,0:T(8,128)}) %reduce-scatter.6.cloned.1.call-update) | async-done | bytes 589840 | tf_op jit(solution)/shard_map/reduce_scatter | solution.py:64
  354.1 2.2 fusion.37
  356.3 0.9 pad_maximum_fusion
  357.2 58.5 %all-gather.2.cloned.1.call-done = bf16[2,576,2048]{2,1,0:T(8,128)(2,1)} async-done(((bf16[2,72,2048]{2,1,0:T(8,128)(2,1)}), bf16[2,576,2048]{2,1,0:T(8,128)(2,1)}) %all-gather.2.cloned.1.call-update) | async-done | bytes 4718608 | tf_op jit(solution)/shard_map/all_gather | solution.py:68
  415.7 5.5 %fusion = f32[576,896]{1,0:T(8,128)S(1)} fusion(bf16[1,896,2048]{2,1,0:T(8,128)(2,1)} %param.14, bf16[2,576,2048]{2,1,0:T(8,128)(2,1)} %all-gather.2.cloned.1.call-done), kind=kOutput, calls=%fused_computation.3 | convolution fusion | flops 2113929216 | bytes 8093696 | tf_op jit(solution)/shard_map/dot_general | solution.py:19
  421.3 2.7 add_convert_fusion
  423.9 1.3 reshape.81
  425.2 7.5 %all-to-all-start.2 = ((bf16[32,18,896]{2,1,0:T(8,128)(2,1)}), bf16[32,18,896]{2,1,0:T(8,128)(2,1)S(1)}, u32[]{:S(2)}, u32[]{:S(2)}) async-start(bf16[32,18,896]{2,1,0:T(8,128)(2,1)} %reshape.81), calls=%async_computation.7 | async-start | bytes 2752512 | tf_op jit(solution)/shard_map/all_to_all | solution.py:71
  432.7 0.1 copy.10
  432.8 20.4 %all-to-all-done.2 = bf16[32,18,896]{2,1,0:T(8,128)(2,1)S(1)} async-done(((bf16[32,18,896]{2,1,0:T(8,128)(2,1)}), bf16[32,18,896]{2,1,0:T(8,128)(2,1)S(1)}, u32[]{:S(2)}, u32[]{:S(2)}) %all-to-all-start.2) | async-done | bytes 1032224 | tf_op jit(solution)/shard_map/all_to_all | solution.py:71
  453.2 0.3 reshape.82
  453.6 2.1 gather_fusion
  455.6 1.3 fusion.14
  (21 shorter events, 0.2 us)
Async XLA Ops:
  6.5 3.4 copy-start
  6.5 118.8 %reduce-scatter.12.cloned.1.call-start = ((), (), s32[]{:S(2)}) async-start(), calls=%async_computation.11 | async-start | bytes 5308416 | tf_op jit(solution)/shard_map/reduce_scatter | solution.py:61
  49.2 120.8 %reduce-scatter.8.cloned.1.call-start = ((), (), s32[]{:S(2)}) async-start(), calls=%async_computation.9 | async-start | bytes 5308416 | tf_op jit(solution)/shard_map/reduce_scatter | solution.py:60
  55.6 0.9 copy-start.1
  55.6 1.0 copy-start.2
  55.6 175.8 %reduce-scatter.10.cloned.1.call-start = ((), (), s32[]{:S(2)}) async-start(), calls=%async_computation.10 | async-start | bytes 5308416 | tf_op jit(solution)/shard_map/reduce_scatter | solution.py:62
  112.3 180.5 %reduce-scatter.14.cloned.1.call-start = ((), (), s32[]{:S(2)}) async-start(), calls=%async_computation.12 | async-start | bytes 5308416 | tf_op jit(solution)/shard_map/reduce_scatter | solution.py:63
  118.9 235.2 %reduce-scatter.6.cloned.1.call-start = ((), (), s32[]{:S(2)}) async-start(), calls=%async_computation.8 | async-start | bytes 5308416 | tf_op jit(solution)/shard_map/reduce_scatter | solution.py:64
  125.3 290.4 %all-gather.2.cloned.1.call-start = ((), (), s32[]{:S(2)}) async-start(), calls=%async_computation.13 | async-start | bytes 5308416 | tf_op jit(solution)/shard_map/all_gather | solution.py:68
  415.7 5.5 %copy-start.4 = (bf16[2,576,2048]{2,1,0:T(8,128)(2,1)S(1)}, bf16[2,576,2048]{2,1,0:T(8,128)(2,1)}, u32[]{:S(2)}) copy-start(bf16[2,576,2048]{2,1,0:T(8,128)(2,1)} %all-gather.2.cloned.1.call-done) | copy-start | bytes 14155780
  415.7 5.5 %copy-start.5 = (bf16[1,896,2048]{2,1,0:T(8,128)(2,1)S(1)}, bf16[1,896,2048]{2,1,0:T(8,128)(2,1)}, u32[]{:S(2)}) copy-start(bf16[1,896,2048]{2,1,0:T(8,128)(2,1)} %param.13) | copy-start | bytes 11010052
  423.9 8.8 %copy-start.3 = (f32[64,8]{0,1:T(8,128)S(1)}, f32[64,8]{0,1:T(8,128)}, u32[]{:S(2)}) copy-start(f32[64,8]{0,1:T(8,128)} %param.12) | copy-start | bytes 6148
  425.2 28.0 %all-to-all-start.2 = ((bf16[32,18,896]{2,1,0:T(8,128)(2,1)}), bf16[32,18,896]{2,1,0:T(8,128)(2,1)S(1)}, u32[]{:S(2)}, u32[]{:S(2)}) async-start(bf16[32,18,896]{2,1,0:T(8,128)(2,1)} %reshape.81), calls=%async_computation.7 | async-start | bytes 2752512 | tf_op jit(solution)/shard_map/all_to_all | solution.py:71
Sparse Core Ops, SparseCore 0:
  49.3 59.1 reduce-scatter.11
  111.0 58.8 reduce-scatter.7
  172.5 58.8 reduce-scatter.9
  233.9 58.8 reduce-scatter.13
  295.2 58.8 reduce-scatter.5
  357.3 58.3 all-gather.1
where the time goes:
time: 464 us
  waiting for transfers between devices  308 us (66%)
  blocking collectives  68.4 us (15%)
  matrix products  39.8 us (9%)
  local copies, waits for them, and re-layouts  19.9 us (4%)
  between operations  13.6 us (3%)
  starting transfers between devices  7.92 us (2%)
  other arithmetic  6.42 us (1%)
    reduce_scatter x1, waiting for transfers between devices, shards(): lax.psum_scatter(part_tgate, 'dp', scatter_dimension=0, tiled=True)  61.5 us
    reduce_scatter x1, waiting for transfers between devices, shards(): lax.psum_scatter(part_tup, 'dp', scatter_dimension=0, tiled=True)  61.3 us
    reduce_scatter x1, waiting for transfers between devices, shards(): lax.psum_scatter(part_back, 'dp', scatter_dimension=0, tiled=True)  61.3 us
    all_gather x1, waiting for transfers between devices, shards(): piece = lax.all_gather(factors, 'dp', axis=1, tiled=True)  58.5 us
    reduce_scatter x1, waiting for transfers between devices, shards(): lax.psum_scatter(part_gate, 'dp', scatter_dimension=0, tiled=True)  44.6 us
    all_to_all x1, blocking collectives, shards(): lax.all_to_all(scatter_rows(paired), 'expert', split_axis=0, concat_axis=...  39.1 us
    all_to_all x1, blocking collectives, shards(): lax.all_to_all(scatter_rows(tokens), 'expert', split_axis=0, concat_axis=...  29.3 us
    all_to_all x1, waiting for transfers between devices, shards(): lax.all_to_all(outgoing, 'expert', split_axis=0, concat_axis=0, tiled=True)  20.4 us
  transfers between devices with their start and end apart: 7, of which 6 were waited for; matrix products, arithmetic and copies ran while one was open for 8% of the time, Pallas kernels for 0%

commit v1 on v0

v1 whole, which is shorter than its diff:
```python
import jax
import jax.numpy as jnp
from jax import lax
from jax.experimental import pallas as pl
from jax.experimental.pallas import tpu as pltpu
from jax.sharding import PartitionSpec as P

MESH = pl.DeviceIdType.MESH
BF16 = jnp.bfloat16
F32 = jnp.float32

TOP = 8
TOK = 64
CAP = 18
DC = 896
H = 2048
NZ = 8
CH = H // NZ
NG = 4
SRC = 8
GR = SRC * CAP
SUMS = 5
MR = SUMS * GR + 16
BR = 3 * TOK + 16
PAD = 32


def nt(a, b):
    return lax.dot_general(a, b, (((1,), (1,)), ((), ())), preferred_element_type=F32)


def nn(a, b):
    return jnp.dot(a, b, preferred_element_type=F32)


def kernel(
    x_ref, v_ref, c_ref, rt_ref, routing_ref, gw_ref, gate_ref, up_ref, down_ref, out_ref,
    gate_v, up_v, down_v, tok, xrows, part, rs_s, rs_r, fac, acc, sbuf, rbuf, wmat,
    w_sem, l_sem, y_ss, y_rs, x_ss, x_rs, x3_ss, x3_rs, sib_ss, sib_rs,
    rs_ss, rs_rs, ag_ss, ag_rs, rt_ss, rt_rs,
):
    me = lax.axis_index("dp")
    ex = lax.axis_index("expert")
    px = ex // 8
    py = (ex // 2) % 4
    pc = ex % 2

    def at_xy(dx, dy, dc):
        return (me, (((px + dx) % 4) * 4 + (py + dy) % 4) * 2 + (pc + dc) % 2)

    z_dev = ((me + NZ - 1) % NZ, ex), ((me + 1) % NZ, ex)
    y_dev = at_xy(0, 1, 0), at_xy(0, 3, 0)
    x_dev = at_xy(1, 0, 0), at_xy(3, 0, 0)
    sib_dev = at_xy(0, 0, 1)

    def remote(src, dst, ss, rs, dev):
        return pltpu.make_async_remote_copy(
            src_ref=src, dst_ref=dst, send_sem=ss, recv_sem=rs, device_id=dev, device_id_type=MESH
        )

    loads = [
        pltpu.make_async_copy(x_ref, tok.at[0, 0, 0, pl.ds(0, TOK)], l_sem.at[0]),
        pltpu.make_async_copy(v_ref, tok.at[0, 0, 0, pl.ds(TOK, TOK)], l_sem.at[1]),
        pltpu.make_async_copy(c_ref, tok.at[0, 0, 0, pl.ds(2 * TOK, TOK)], l_sem.at[2]),
        pltpu.make_async_copy(rt_ref, tok.at[0, 0, 0, pl.ds(3 * TOK, 16)], l_sem.at[3]),
    ]
    weights = [
        pltpu.make_async_copy(gate_ref, gate_v, w_sem.at[0]),
        pltpu.make_async_copy(up_ref, up_v, w_sem.at[1]),
        pltpu.make_async_copy(down_ref, down_v, w_sem.at[2]),
    ]
    for cp in loads:
        cp.start()
    for cp in weights:
        cp.start()

    bar = pltpu.get_barrier_semaphore()
    for d in (0, 1):
        pl.semaphore_signal(bar, 1, device_id=z_dev[d], device_id_type=MESH)

    def greet(o, _):
        pl.semaphore_signal(bar, 1, device_id=(me, (ex + o) % 32), device_id_type=MESH)
        return 0

    lax.fori_loop(1, 32, greet, 0)
    pl.semaphore_wait(bar, 33)

    def y_copy(i):
        if i == 0:
            return remote(tok.at[0, 0, 0], tok.at[0, 0, 3], y_ss.at[0], y_rs.at[0], y_dev[0])
        if i == 1:
            return remote(tok.at[0, 0, 0], tok.at[0, 0, 1], y_ss.at[1], y_rs.at[1], y_dev[1])
        if i == 2:
            rows = pl.ds(0, 96)
            return remote(tok.at[0, 0, 3, rows], tok.at[0, 0, 2, rows], y_ss.at[2], y_rs.at[2], y_dev[0])
        rows = pl.ds(96, BR - 96)
        return remote(tok.at[0, 0, 1, rows], tok.at[0, 0, 2, rows], y_ss.at[3], y_rs.at[3], y_dev[1])

    def x_copy(d, dy):
        return remote(
            tok.at[0, 0, dy], tok.at[2 - d, 0, dy], x_ss.at[d * 4 + dy], x_rs.at[d * 4 + dy], x_dev[d]
        )

    def x3_copy(dy):
        g, d = (1, 1) if dy < 2 else (2, 0)
        return remote(tok.at[g, 0, dy], tok.at[3, 0, dy], x3_ss.at[dy], x3_rs.at[dy], x_dev[d])

    def sib_copy(g, dy):
        return remote(
            tok.at[g, 0, dy], tok.at[g, 1, dy], sib_ss.at[g * 4 + dy], sib_rs.at[g * 4 + dy], sib_dev
        )

    def rs_copy(g, d, k, h):
        s = (((g % 2) * 2 + d) * 4 + k) * 2 + h
        r = ((g * 2 + d) * 4 + k) * 2 + h
        return remote(rs_s.at[s], rs_r.at[r], rs_ss.at[s], rs_rs.at[r], z_dev[d])

    def ag_copy(g, d, k, h):
        i = ((g * 2 + d) * 4 + k) * 2 + h
        src, dst = (k, k + 1) if d == 0 else ((8 - k) % 8, 7 - k)
        return remote(
            fac.at[(g * 8 + src) * 2 + h], fac.at[(g * 8 + dst) * 2 + h], ag_ss.at[i], ag_rs.at[i], z_dev[d]
        )

    def dx_of(g):
        return g + g // 2 - 2 * (g // 3)

    def back_copy(g, j):
        dev = at_xy(dx_of(g), j % 4, j // 4)
        return remote(sbuf.at[g * SRC + j], rbuf.at[ex], rt_ss.at[g * SRC + j], rt_rs.at[ex], dev)

    def gather(g):
        lane = lax.broadcasted_iota(jnp.int32, (8, 128), 1)
        tri_r = lax.broadcasted_iota(jnp.int32, (128, 128), 0)
        tri_c = lax.broadcasted_iota(jnp.int32, (128, 128), 1)
        tri = ((tri_r < tri_c) & (tri_r // 64 == tri_c // 64)).astype(F32).astype(BF16)
        row = lax.broadcasted_iota(jnp.int32, (GR, 128), 0).astype(F32)
        low = lax.broadcasted_iota(jnp.int32, (16, 128), 1) < 64
        exf = ex.astype(F32)
        hots = []
        for c in range(2):
            for p in range(2):
                ra = tok[g, c, 2 * p, pl.ds(3 * TOK, 16), pl.ds(0, 128)].astype(F32)
                rb = tok[g, c, 2 * p + 1, pl.ds(3 * TOK, 16), pl.ds(0, 128)].astype(F32)
                hit = jnp.where(jnp.where(low, ra, rb) == exf, 1.0, 0.0)
                hit = jnp.broadcast_to(jnp.sum(hit, axis=0, keepdims=True), (8, 128))
                rank = nn(hit.astype(BF16), tri)
                first = (CAP * (4 * c + 2 * p) + CAP * (lane // 64)).astype(F32)
                target = jnp.where(hit > 0.5, rank + first, -1.0)
                hots.append(jnp.where(row == target[0:1], 1.0, 0.0).astype(BF16))
        hot = jnp.concatenate(hots, axis=1)
        for a in range(3):
            rows = jnp.concatenate(
                [tok[g, c, y, pl.ds(a * TOK, TOK), :] for c in range(2) for y in range(4)], axis=0
            )
            xrows[g % 2, pl.ds(a * GR, GR), :] = nn(hot, rows).astype(BF16)

    def products(g, d, chunk):
        first = pl.multiple_of(chunk * CH, CH)
        cols = pl.ds(first, CH)
        xv = xrows[g % 2, pl.ds(0, 2 * GR), :]
        part[d, pl.ds(0, 2 * GR), :] = nn(xv, gate_v[:, cols])
        part[d, pl.ds(2 * GR, 2 * GR), :] = nn(xv, up_v[:, cols])
        part[d, pl.ds(4 * GR, GR), :] = nt(xrows[g % 2, pl.ds(2 * GR, GR), :], down_v[cols, :])

    def scales(r):
        return jnp.exp2(rs_r[r, pl.ds(SUMS * GR, 16), :].astype(F32) * (1.0 / 256.0))

    def send_sums(g, d, k, h, came):
        s = (((g % 2) * 2 + d) * 4 + k) * 2 + h
        own = 0 if k == 0 else d

        @pl.when(g >= 2)
        def _():
            rs_copy(g, d, k, h).wait_send()

        r = ((g * 2 + d) * 4 + k - 1) * 2 + h
        if came:
            rs_copy(g, d, k - 1, h).wait_recv()
            sc = scales(r)
        codes = jnp.zeros((16, 128), F32)
        at = lax.broadcasted_iota(jnp.int32, (16, 128), 0)
        for p in range(SUMS):
            rows = pl.ds(p * GR, GR)
            blk = part[own, rows, pl.ds(h * 128, 128)]
            if came:
                blk = blk + rs_r[r, rows, :].astype(F32) * sc[p : p + 1]
            most = jnp.max(jnp.abs(blk), axis=0, keepdims=True)
            code = jnp.ceil(256.0 * jnp.log2(jnp.maximum(most, 1e-30) * (1.0 / 32760.0)))
            inv = jnp.exp2(code * (-1.0 / 256.0))
            rs_s[s, rows, :] = jnp.round(blk * inv).astype(jnp.int32).astype(jnp.int16)
            codes = jnp.where(at == p, code, codes)
        rs_s[s, pl.ds(SUMS * GR, 16), :] = codes.astype(jnp.int32).astype(jnp.int16)
        rs_copy(g, d, k, h).start()

    def stage_0(g):
        products(g, 0, (me + 4) % NZ)
        for d in (0, 1):
            send_sums(g, d, 0, d, False)

    def stage(g, k):
        products(g, 0, (me + NZ - (4 - k)) % NZ)
        products(g, 1, (me + 4 - k) % NZ)
        if k == 1:
            send_sums(g, 0, 1, 1, False)
            send_sums(g, 1, 1, 0, False)
            send_sums(g, 0, 1, 0, True)
            send_sums(g, 1, 1, 1, True)
        else:
            for h in (1, 0):
                for d in (0, 1):
                    send_sums(g, d, k, h if d == 0 else 1 - h, True)

    def stage_4(g):
        products(g, 0, me)
        for h in (0, 1):
            total = []
            r = [((g * 2 + d) * 4 + 3) * 2 + h for d in (0, 1)]
            for d in (0, 1):
                rs_copy(g, d, 3, h).wait_recv()
            sc = [scales(r[0]), scales(r[1])]
            for p in range(SUMS):
                rows = pl.ds(p * GR, GR)
                blk = part[0, rows, pl.ds(h * 128, 128)]
                for d in (0, 1):
                    blk = blk + rs_r[r[d], rows, :].astype(F32) * sc[d][p : p + 1]
                total.append(blk)
            a, da, b, db, dh = total
            sig = 1.0 / (1.0 + jnp.exp(-a))
            s1 = sig * (1.0 + a * (1.0 - sig))
            s2 = sig * (1.0 - sig) * (2.0 + a * (1.0 - 2.0 * sig))
            fac[g * 16 + h, pl.ds(0, GR), :] = (dh * (s2 * da * b + s1 * db)).astype(BF16)
            fac[g * 16 + h, pl.ds(GR, GR), :] = (dh * s1 * da).astype(BF16)
            for d in (0, 1):
                ag_copy(g, d, 0, h).start()

    def add_rows(g, r, new):
        cols = pl.ds(pl.multiple_of(((me + r) % NZ) * CH, CH), CH)
        f = jnp.concatenate([fac[(g * 8 + r) * 2], fac[(g * 8 + r) * 2 + 1]], axis=1)
        more = nt(f[0:GR], gate_v[:, cols]) + nt(f[GR:], up_v[:, cols])
        acc[...] = more if new else acc[...] + more

    def gather_stage(g, k):
        for h in (0, 1):
            for d in (0, 1):
                ag_copy(g, d, k - 1, h).wait_recv()
                if k < 3 or h == d:
                    ag_copy(g, d, k, h).start()
        if k == 1:
            add_rows(g, 0, True)
        add_rows(g, k, False)
        add_rows(g, 8 - k, False)

    def last_stage(g):
        ag_copy(g, 0, 3, 0).wait_recv()
        ag_copy(g, 1, 3, 1).wait_recv()
        add_rows(g, 4, False)
        rows = acc[...].astype(BF16)
        o = lax.broadcasted_iota(jnp.int32, (SRC * PAD, GR), 0)
        i = lax.broadcasted_iota(jnp.int32, (SRC * PAD, GR), 1)
        hot = jnp.where((o % PAD < CAP) & (i == (o // PAD) * CAP + o % PAD), 1.0, 0.0).astype(BF16)
        spread = nn(hot, rows).astype(BF16)
        for j in range(SRC):
            sbuf[g * SRC + j] = spread[j * PAD : (j + 1) * PAD]
        for j in range(SRC):
            if j == 0:

                @pl.when(g == 0)
                def _():
                    pltpu.make_async_copy(sbuf.at[0], rbuf.at[ex], rt_rs.at[ex]).start()

                @pl.when(g > 0)
                def _():
                    back_copy(g, 0).start()
            else:
                back_copy(g, j).start()

    for cp in loads:
        cp.wait()
    y_copy(0).start()
    y_copy(1).start()
    sib_copy(0, 0).start()
    x_copy(0, 0).start()
    x_copy(1, 0).start()

    hits = jnp.zeros((TOK, 128), F32)
    lane = lax.broadcasted_iota(jnp.int32, (TOK, 128), 1)
    for k in range(TOP):
        hits = hits + jnp.where(routing_ref[:, k : k + 1] == lane, 1.0, 0.0)
    tri = lax.broadcasted_iota(jnp.int32, (TOK, TOK), 1) < lax.broadcasted_iota(jnp.int32, (TOK, TOK), 0)
    place = nn(jnp.where(tri, 1.0, 0.0).astype(BF16), hits.astype(BF16)) + (lane * PAD).astype(F32)
    col = lax.broadcasted_iota(jnp.int32, (TOK, 32 * PAD), 1).astype(F32)
    w = jnp.zeros((TOK, 32 * PAD), F32)
    for k in range(TOP):
        at = jnp.sum(jnp.where(routing_ref[:, k : k + 1] == lane, place, 0.0), axis=1, keepdims=True)
        w = w + jnp.where(col == at, gw_ref[:, k : k + 1], 0.0)
    for i in range(3):
        piece = w.astype(BF16)
        wmat[pl.ds(i * TOK, TOK), :] = piece
        w = w - piece.astype(F32)

    y_copy(1).wait_recv()
    y_copy(3).start()
    y_copy(0).wait_recv()
    y_copy(2).start()
    for dy in (1, 3):
        sib_copy(0, dy).start()
        x_copy(0, dy).start()
        x_copy(1, dy).start()
    y_copy(2).wait_recv()
    y_copy(3).wait_recv()
    sib_copy(0, 2).start()
    x_copy(0, 2).start()
    x_copy(1, 2).start()
    for cp in weights:
        cp.wait()
    for dy in (0, 1, 3, 2):
        sib_copy(0, dy).wait_recv()
    gather(0)
    stage_0(0)

    def turn(i, _):
        for k in (1, 2, 3):

            @pl.when(i < NG)
            def _():
                stage(i, k)

            @pl.when(i >= 1)
            def _():
                gather_stage(i - 1, k)

        @pl.when(i == 0)
        def _():
            for dy in range(4):
                for d in (1, 0):
                    x_copy(d, dy).wait_recv()
                    sib_copy(2 - d, dy).start()
            for dy in range(4):
                x3_copy(dy).start()
            for dy in range(4):
                sib_copy(1, dy).wait_recv()

        @pl.when(i == 1)
        def _():
            for dy in range(4):
                x3_copy(dy).wait_recv()
                sib_copy(3, dy).start()
            for dy in range(4):
                sib_copy(2, dy).wait_recv()

        @pl.when(i == 2)
        def _():
            for dy in range(4):
                sib_copy(3, dy).wait_recv()

        @pl.when(i < NG - 1)
        def _():
            gather(i + 1)
            stage_0(i + 1)

        @pl.when(i >= 1)
        def _():
            last_stage(i - 1)

        @pl.when(i < NG)
        def _():
            stage_4(i)

        return 0

    lax.fori_loop(0, NG + 1, turn, 0)

    def arrive(e, _):
        pltpu.make_async_copy(rbuf.at[e], rbuf.at[e], rt_rs.at[e]).wait()
        return 0

    lax.fori_loop(0, 32, arrive, 0)
    parts = nn(wmat[...], jnp.concatenate([rbuf[e] for e in range(32)], axis=0))
    out_ref[...] = parts[2 * TOK :] + parts[TOK : 2 * TOK] + parts[:TOK]

    for i in range(4):
        y_copy(i).wait_send()
        x3_copy(i).wait_send()
        for d in (0, 1):
            x_copy(d, i).wait_send()
        for g in range(NG):
            sib_copy(g, i).wait_send()

    def left(g, _):
        for d in (0, 1):
            for k in range(4):
                for h in (0, 1):
                    if k > 0 or h == d:

                        @pl.when(g >= 2)
                        def _():
                            rs_copy(g, d, k, h).wait_send()

                    if k < 3 or h == d:
                        ag_copy(g, d, k, h).wait_send()
        for j in range(SRC):
            if j == 0:

                @pl.when(g > 0)
                def _():
                    back_copy(g, 0).wait_send()
            else:
                back_copy(g, j).wait_send()
        return 0

    lax.fori_loop(0, NG, left, 0)


def shards(tokens, tangent, cotangent, routing, gate_weights, gate_proj, up_proj, down_proj):
    names = routing.T.astype(BF16)
    names = jnp.concatenate([names, names], axis=1)
    names = jnp.pad(names, ((0, 8), (0, DC - 128)), constant_values=-1.0)
    dma = pltpu.SemaphoreType.DMA
    anywhere = pl.BlockSpec(memory_space=pl.ANY)
    vmem = pl.BlockSpec(memory_space=pltpu.VMEM)
    return pl.pallas_call(
        kernel,
        out_shape=jax.ShapeDtypeStruct((TOK, DC), F32),
        in_specs=[anywhere] * 4 + [vmem] * 2 + [anywhere] * 3,
        out_specs=vmem,
        scratch_shapes=[
            pltpu.VMEM((DC, H), BF16),
            pltpu.VMEM((DC, H), BF16),
            pltpu.VMEM((H, DC), BF16),
            pltpu.VMEM((NG, 2, 4, BR, DC), BF16),
            pltpu.VMEM((2, 3 * GR, DC), BF16),
            pltpu.VMEM((2, SUMS * GR, CH), F32),
            pltpu.VMEM((32, MR, 128), jnp.int16),
            pltpu.VMEM((64, MR, 128), jnp.int16),
            pltpu.VMEM((NG * 16, 2 * GR, 128), BF16),
            pltpu.VMEM((GR, DC), F32),
            pltpu.VMEM((NG * SRC, PAD, DC), BF16),
            pltpu.VMEM((32, PAD, DC), BF16),
            pltpu.VMEM((3 * TOK, 32 * PAD), BF16),
            dma((3,)), dma((4,)), dma((4,)), dma((4,)), dma((8,)), dma((8,)), dma((4,)), dma((4,)),
            dma((16,)), dma((16,)), dma((32,)), dma((64,)), dma((64,)), dma((64,)), dma((32,)), dma((32,)),
        ],
        compiler_params=pltpu.CompilerParams(
            collective_id=0, has_side_effects=True, vmem_limit_bytes=61 * 1024 * 1024
        ),
        cost_estimate=pl.CostEstimate(
            flops=2 * 7 * 576 * DC * H, bytes_accessed=12_000_000, transcendentals=576 * H // NZ
        ),
    )(tokens, tangent, cotangent, names, routing, gate_weights, gate_proj[0], up_proj[0], down_proj[0])


def solution(mesh):
    in_specs = (
        P("expert", "dp"),
        P("expert", "dp"),
        P("expert", "dp"),
        P("expert", None),
        P("expert", None),
        P("expert", "dp", None),
        P("expert", "dp", None),
        P("expert", None, "dp"),
    )
    return jax.shard_map(
        shards, mesh=mesh, in_specs=in_specs, out_specs=P("expert", "dp"), check_vma=False
    )
```

time: 464 us -> 218 us (0.47)
  waiting for transfers between devices: 308 us -> 0 us
  Pallas kernels: 0 us -> 212 us
  blocking collectives: 68.4 us -> 0 us
  matrix products: 39.8 us -> 0 us
  local copies, waits for them, and re-layouts: 19.9 us -> 4.4 us
  between operations: 13.6 us -> 0.01 us
  starting transfers between devices: 7.92 us -> 0 us
  other arithmetic: 6.42 us -> 1.36 us
    reduce_scatter x5 -> x0, waiting for transfers between devices: 229 us -> none  [the longest x1 61.5 us: shards(): lax.psum_scatter(part_tgate, 'dp', scatter_dimension=0, tiled=True)]
    pallas_call x0 -> x1, Pallas kernels: none -> 212 us  [shards(): pl.pallas_call(kernel, out_shape=jax.ShapeDtypeStruct((TOK, DC), F32), in...]
    all_to_all x2 -> x0, blocking collectives: 68.4 us -> none  [the longest x1 39.1 us: shards(): lax.all_to_all(scatter_rows(paired), 'expert', split_axis=0, concat_axis=...]
    all_gather x1 -> x0, waiting for transfers between devices: 58.5 us -> none  [shards(): piece = lax.all_gather(factors, 'dp', axis=1, tiled=True)]
    dot_general x7 -> x0, matrix products: 39.8 us -> none  [the longest x3 14.5 us: contract_last(): lax.dot_general(left_rows, right_matrix, (((1,), (1,)), ((), ())), prefer...]
    all_to_all x1 -> x0, waiting for transfers between devices: 20.4 us -> none  [shards(): lax.all_to_all(outgoing, 'expert', split_axis=0, concat_axis=0, tiled=True)]
    scatter x2 -> x0, local copies, waits for them, and re-layouts: 7.74 us -> none  [scatter_rows(): zero_buf.at[target_row].set(spread)]
    reshape x6 -> x0, local copies, waits for them, and re-layouts: 7.72 us -> none  [the longest x2 2.94 us: scatter_rows(): zero_buf.at[target_row].set(spread)]
  transfers between devices with their start and end apart: 7 -> 0, of which waited for: 6 -> 0; matrix products, arithmetic and copies ran while one was open for 8% -> 0% of each run, Pallas kernels for 0% -> 0%
where the time goes in v1:
time: 218 us; the launch traced here: 217 us
  Pallas kernels  212 us (97%)
  local copies, waits for them, and re-layouts  4.4 us (2%)
    pallas_call x1, Pallas kernels, shards(): pl.pallas_call(kernel, out_shape=jax.ShapeDtypeStruct((TOK, DC), F32), in...  212 us
    unnamed x3, local copies, waits for them, and re-layouts  4.4 us

profile of v1, /device:TPU:1, one launch (start us, length us, event | category | flops | bytes accessed | tf_op | source)
XLA Modules:
  0.0 217.3 jit_solution(6017797085097860488)
XLA Ops:
  0.0 0.7 convert_bitcast_fusion
  0.7 0.7 fusion.5.rt_ref
  1.4 1.4 copy.10.gw_ref
  2.7 1.4 copy.9.routing_ref
  4.1 211.6 %shard_map.82 = f32[64,896]{1,0:T(8,128)} custom-call(bf16[64,896]{1,0:T(8,128)(2,1)} %x_ref.1, bf16[64,896]{1,0:T(8,128)(2,1)} %v_ref.1, bf16[64,896]{1,0:T(8,128)(2,1)} %c_ref.1, bf16[16,896]{1,0:T(8,128)(2,1)} %fusion.5.rt_ref, s32[64,8]{1,0:T(8,128)} %copy.9.routing_ref, f32[64,8]{1,0:T(8,128)} %copy.10.gw_ref, bf16[896,2048]{1,0:T(8,128)(2,1)} %bitcast.5, ...), custom_call_target="tpu_custom_call" | custom-call | flops 14797504512 | bytes 12000000 | tf_op jit(solution)/shard_map/pallas_call | solution.py:422
  215.7 1.6 copy.12

commit v2 on v1

v2 whole, which is shorter than its diff:
```python
import jax
import jax.numpy as jnp
from jax import lax
from jax.experimental import pallas as pl
from jax.experimental.pallas import tpu as pltpu
from jax.sharding import PartitionSpec as P

MESH = pl.DeviceIdType.MESH
BF16 = jnp.bfloat16
F32 = jnp.float32

TOP = 8
TOK = 64
CAP = 18
DC = 896
H = 2048
NZ = 8
CH = H // NZ
NG = 4
SRC = 8
GR = SRC * CAP
SUMS = 5
CHIPS = (
    ((0, 0), (0, 1), (1, 0), (0, 3)),
    ((3, 0), (0, 2), (2, 0), (3, 2)),
    ((1, 2), (2, 1), (2, 3), (2, 2)),
    ((1, 1), (1, 3), (3, 1), (3, 3)),
)
MR = SUMS * GR + 16
BR = 16 + 3 * TOK
PARTS = (pl.ds(0, 16 + TOK), pl.ds(16 + TOK, 2 * TOK))
PAD = 32


def nt(a, b):
    return lax.dot_general(a, b, (((1,), (1,)), ((), ())), preferred_element_type=F32)


def nn(a, b):
    return jnp.dot(a, b, preferred_element_type=F32)


def kernel(
    x_ref, v_ref, c_ref, routing_ref, gw_ref, gate_ref, up_ref, down_ref, out_ref,
    gate_v, up_v, down_v, tok, xrows, part, rs_s, rs_r, fac, acc, sbuf, rbuf, wmat,
    w_sem, l_sem, y_ss, y_rs, x_ss, x_rs, x3_ss, x3_rs, sib_ss, sib_rs,
    rs_ss, rs_rs, ag_ss, ag_rs, rt_ss, rt_rs,
):
    me = lax.axis_index("dp")
    ex = lax.axis_index("expert")
    px = ex // 8
    py = (ex // 2) % 4
    pc = ex % 2

    def at_xy(dx, dy, dc):
        return (me, (((px + dx + 4) % 4) * 4 + (py + dy + 4) % 4) * 2 + (pc + dc) % 2)

    z_dev = ((me + NZ - 1) % NZ, ex), ((me + 1) % NZ, ex)
    y_dev = at_xy(0, 1, 0), at_xy(0, 3, 0)
    x_dev = at_xy(1, 0, 0), at_xy(3, 0, 0)
    sib_dev = at_xy(0, 0, 1)

    def remote(src, dst, ss, rs, dev):
        return pltpu.make_async_remote_copy(
            src_ref=src, dst_ref=dst, send_sem=ss, recv_sem=rs, device_id=dev, device_id_type=MESH
        )

    loads = [
        pltpu.make_async_copy(x_ref, tok.at[0, 0, 0, pl.ds(16, TOK)], l_sem.at[0]),
        pltpu.make_async_copy(v_ref, tok.at[0, 0, 0, pl.ds(16 + TOK, TOK)], l_sem.at[1]),
        pltpu.make_async_copy(c_ref, tok.at[0, 0, 0, pl.ds(16 + 2 * TOK, TOK)], l_sem.at[2]),
    ]
    weights = [
        pltpu.make_async_copy(gate_ref, gate_v, w_sem.at[0]),
        pltpu.make_async_copy(up_ref, up_v, w_sem.at[1]),
        pltpu.make_async_copy(down_ref, down_v, w_sem.at[2]),
    ]
    for cp in loads:
        cp.start()
    for cp in weights:
        cp.start()

    bar = pltpu.get_barrier_semaphore()
    for d in (0, 1):
        pl.semaphore_signal(bar, 1, device_id=z_dev[d], device_id_type=MESH)

    def greet(o, _):
        pl.semaphore_signal(bar, 1, device_id=(me, (ex + o) % 32), device_id_type=MESH)
        return 0

    lax.fori_loop(1, 32, greet, 0)

    named = jnp.concatenate([routing_ref[...].astype(F32), jnp.full((8, TOK), -1.0, F32)], axis=0).astype(BF16)
    twice = lax.broadcasted_iota(jnp.int32, (TOK, 128), 1) % TOK == lax.broadcasted_iota(jnp.int32, (TOK, 128), 0)
    tok[0, 0, 0, pl.ds(0, 16), :] = jnp.zeros((16, DC), BF16)
    tok[0, 0, 0, pl.ds(0, 16), pl.ds(0, 128)] = nn(named, jnp.where(twice, 1.0, 0.0).astype(BF16)).astype(BF16)
    pl.semaphore_wait(bar, 33)

    def slot(col, dy):
        return next((g, i) for g in range(NG) for i in range(4) if CHIPS[g][i] == (col, dy))

    def block(col, dy, q=None):
        g, i = slot(col, dy)
        if q is None:
            return tok.at[g, 0, i]
        return tok.at[g, 0, i, PARTS[q]]

    def y_copy(i, q):
        if i == 0:
            return remote(block(0, 0, q), block(0, 3, q), y_ss.at[q], y_rs.at[q], y_dev[0])
        if i == 1:
            return remote(block(0, 0, q), block(0, 1, q), y_ss.at[2 + q], y_rs.at[2 + q], y_dev[1])
        src = block(0, 3, q) if q == 0 else block(0, 1, q)
        return remote(src, block(0, 2, q), y_ss.at[4 + q], y_rs.at[4 + q], y_dev[q])

    def x_copy(d, dy, q=None):
        i = d * 5 + (dy if dy else 4 * (q or 0))
        return remote(block(0, dy, q), block(1 if d else 3, dy, q), x_ss.at[i], x_rs.at[i], x_dev[d])

    def x3_copy(dy):
        col, d = (1, 1) if dy < 2 else (3, 0)
        return remote(block(col, dy), block(2, dy), x3_ss.at[dy], x3_rs.at[dy], x_dev[d])

    def sib_copy(g, i, q=None):
        n = g * 4 + i + (16 if q == 1 else 0)
        rows = pl.ds(0, BR) if q is None else PARTS[q]
        return remote(tok.at[g, 0, i, rows], tok.at[g, 1, i, rows], sib_ss.at[n], sib_rs.at[n], sib_dev)

    def rs_copy(g, d, k, h):
        s = (((g % 2) * 2 + d) * 4 + k) * 2 + h
        r = ((g * 2 + d) * 4 + k) * 2 + h
        return remote(rs_s.at[s], rs_r.at[r], rs_ss.at[s], rs_rs.at[r], z_dev[d])

    def ag_copy(g, d, k, h, q):
        i = (((g * 2 + d) * 4 + k) * 2 + h) * 2 + q
        src, dst = (k, k + 1) if d == 0 else ((8 - k) % 8, 7 - k)
        rows = pl.ds(q * GR, GR)
        return remote(
            fac.at[(g * 8 + src) * 2 + h, rows], fac.at[(g * 8 + dst) * 2 + h, rows], ag_ss.at[i], ag_rs.at[i], z_dev[d]
        )

    def back_copy(g, j):
        dx, dy = CHIPS[g][j % 4]
        n = g * SRC + j
        return remote(sbuf.at[n], rbuf.at[n], rt_ss.at[n], rt_rs.at[n], at_xy(dx, dy, j // 4))

    def gather(g):
        lane = lax.broadcasted_iota(jnp.int32, (8, 128), 1)
        tri_r = lax.broadcasted_iota(jnp.int32, (128, 128), 0)
        tri_c = lax.broadcasted_iota(jnp.int32, (128, 128), 1)
        tri = ((tri_r < tri_c) & (tri_r // 64 == tri_c // 64)).astype(F32).astype(BF16)
        row = lax.broadcasted_iota(jnp.int32, (GR, 128), 0).astype(F32)
        low = lax.broadcasted_iota(jnp.int32, (16, 128), 1) < 64
        exf = ex.astype(F32)
        hots = []
        for c in range(2):
            for p in range(2):
                ra = tok[g, c, 2 * p, pl.ds(0, 16), pl.ds(0, 128)].astype(F32)
                rb = tok[g, c, 2 * p + 1, pl.ds(0, 16), pl.ds(0, 128)].astype(F32)
                hit = jnp.where(jnp.where(low, ra, rb) == exf, 1.0, 0.0)
                hit = jnp.broadcast_to(jnp.sum(hit, axis=0, keepdims=True), (8, 128))
                rank = nn(hit.astype(BF16), tri)
                first = (CAP * (4 * c + 2 * p) + CAP * (lane // 64)).astype(F32)
                target = jnp.where(hit > 0.5, rank + first, -1.0)
                hots.append(jnp.where(row == target[0:1], 1.0, 0.0).astype(BF16))
        hot = jnp.concatenate(hots, axis=1)
        for a in range(3):
            rows = jnp.concatenate(
                [tok[g, c, y, pl.ds(16 + a * TOK, TOK), :] for c in range(2) for y in range(4)], axis=0
            )
            xrows[g % 2, pl.ds(a * GR, GR), :] = nn(hot, rows).astype(BF16)

    def products(g, d, chunk):
        first = pl.multiple_of(chunk * CH, CH)
        cols = pl.ds(first, CH)
        xv = xrows[g % 2, pl.ds(0, 2 * GR), :]
        part[d, pl.ds(0, 2 * GR), :] = nn(xv, gate_v[:, cols])
        part[d, pl.ds(2 * GR, 2 * GR), :] = nn(xv, up_v[:, cols])
        part[d, pl.ds(4 * GR, GR), :] = nt(xrows[g % 2, pl.ds(2 * GR, GR), :], down_v[cols, :])

    def scales(r):
        return jnp.exp2(rs_r[r, pl.ds(SUMS * GR, 16), :].astype(F32) * (1.0 / 256.0))

    def send_sums(g, d, k, h, came):
        s = (((g % 2) * 2 + d) * 4 + k) * 2 + h
        own = 2 if k == 0 else 3 + d if k == 1 else d

        @pl.when(g >= 2)
        def _():
            rs_copy(g, d, k, h).wait_send()

        r = ((g * 2 + d) * 4 + k - 1) * 2 + h
        if came:
            rs_copy(g, d, k - 1, h).wait_recv()
            sc = scales(r)
        codes = jnp.zeros((16, 128), F32)
        at = lax.broadcasted_iota(jnp.int32, (16, 128), 0)
        for p in range(SUMS):
            rows = pl.ds(p * GR, GR)
            blk = part[own, rows, pl.ds(h * 128, 128)]
            if came:
                blk = blk + rs_r[r, rows, :].astype(F32) * sc[p : p + 1]
            most = jnp.max(jnp.abs(blk), axis=0, keepdims=True)
            code = jnp.ceil(256.0 * jnp.log2(jnp.maximum(most, 1e-30) * (1.0 / 32760.0)))
            inv = jnp.exp2(code * (-1.0 / 256.0))
            rs_s[s, rows, :] = jnp.round(blk * inv).astype(jnp.int32).astype(jnp.int16)
            codes = jnp.where(at == p, code, codes)
        rs_s[s, pl.ds(SUMS * GR, 16), :] = codes.astype(jnp.int32).astype(jnp.int16)
        rs_copy(g, d, k, h).start()

    def stage_0(g):
        products(g, 2, (me + 4) % NZ)
        for d in (0, 1):
            send_sums(g, d, 0, d, False)
        products(g, 3, (me + NZ - 3) % NZ)
        products(g, 4, (me + 3) % NZ)
        for d in (0, 1):
            send_sums(g, d, 1, 1 - d, False)

    def stage(g, k):
        if k == 1:
            for d in (0, 1):
                send_sums(g, d, 1, d, True)
            return
        products(g, 0, (me + NZ - (4 - k)) % NZ)
        products(g, 1, (me + 4 - k) % NZ)
        for h in (1, 0):
            for d in (0, 1):
                send_sums(g, d, k, h if d == 0 else 1 - h, True)

    def stage_4(g):
        products(g, 2, me)
        for h in (0, 1):
            total = []
            r = [((g * 2 + d) * 4 + 3) * 2 + h for d in (0, 1)]
            for d in (0, 1):
                rs_copy(g, d, 3, h).wait_recv()
            sc = [scales(r[0]), scales(r[1])]
            for p in range(SUMS):
                rows = pl.ds(p * GR, GR)
                blk = part[2, rows, pl.ds(h * 128, 128)]
                for d in (0, 1):
                    blk = blk + rs_r[r[d], rows, :].astype(F32) * sc[d][p : p + 1]
                total.append(blk)
            a, da, b, db, dh = total
            sig = 1.0 / (1.0 + jnp.exp(-a))
            s1 = sig * (1.0 + a * (1.0 - sig))
            s2 = sig * (1.0 - sig) * (2.0 + a * (1.0 - 2.0 * sig))
            fac[g * 16 + h, pl.ds(0, GR), :] = (dh * (s2 * da * b + s1 * db)).astype(BF16)
            fac[g * 16 + h, pl.ds(GR, GR), :] = (dh * s1 * da).astype(BF16)
            for q in (0, 1):
                for d in (0, 1):
                    ag_copy(g, d, 0, h, q).start()

    def add_rows(g, r, new):
        cols = pl.ds(pl.multiple_of(((me + r) % NZ) * CH, CH), CH)
        f = jnp.concatenate([fac[(g * 8 + r) * 2], fac[(g * 8 + r) * 2 + 1]], axis=1)
        more = nt(f[0:GR], gate_v[:, cols]) + nt(f[GR:], up_v[:, cols])
        acc[...] = more if new else acc[...] + more

    def gather_stage(g, k):
        for h in (0, 1):
            for q in (0, 1):
                for d in (0, 1):
                    ag_copy(g, d, k - 1, h, q).wait_recv()
                    if k < 3 or h == d:
                        ag_copy(g, d, k, h, q).start()
        if k == 1:
            add_rows(g, 0, True)
        add_rows(g, k, False)
        add_rows(g, 8 - k, False)

    def last_stage(g):
        for q in (0, 1):
            for d in (0, 1):
                ag_copy(g, d, 3, d, q).wait_recv()
        add_rows(g, 4, False)
        rows = acc[...].astype(BF16)
        o = lax.broadcasted_iota(jnp.int32, (SRC * PAD, GR), 0)
        i = lax.broadcasted_iota(jnp.int32, (SRC * PAD, GR), 1)
        hot = jnp.where((o % PAD < CAP) & (i == (o // PAD) * CAP + o % PAD), 1.0, 0.0).astype(BF16)
        spread = nn(hot, rows).astype(BF16)
        for j in range(SRC):
            sbuf[g * SRC + j] = spread[j * PAD : (j + 1) * PAD]
        for at in range(NG):

            @pl.when(g == at)
            def _():
                for j in range(SRC):
                    if at == 0 and j == 0:
                        pltpu.make_async_copy(sbuf.at[0], rbuf.at[0], rt_rs.at[0]).start()
                    else:
                        back_copy(at, j).start()

    loads[0].wait()
    for q in (0, 1):
        if q == 1:
            loads[1].wait()
            loads[2].wait()
        y_copy(0, q).start()
        y_copy(1, q).start()
        x_copy(1, 0, q).start()
        sib_copy(0, 0, q).start()
        x_copy(0, 0, q).start()

    same = lax.broadcasted_iota(jnp.int32, (TOK, TOK), 0) == lax.broadcasted_iota(jnp.int32, (TOK, TOK), 1)
    same = jnp.where(same, 1.0, 0.0).astype(BF16)
    names = nt(same, routing_ref[...].astype(F32).astype(BF16))
    rest = gw_ref[...]
    gw = jnp.zeros((TOK, TOP), F32)
    for i in range(3):
        piece = rest.astype(BF16)
        gw = gw + nt(same, piece)
        rest = rest - piece.astype(F32)
    hits = jnp.zeros((TOK, 128), F32)
    lane = lax.broadcasted_iota(jnp.int32, (TOK, 128), 1).astype(F32)
    for k in range(TOP):
        hits = hits + jnp.where(names[:, k : k + 1] == lane, 1.0, 0.0)
    order = jnp.zeros((TOK, 128), F32)
    for n in range(NG * SRC):
        dx, dy = CHIPS[n // SRC][n % 4]
        order = jnp.where(lane == at_xy(-dx, -dy, n % SRC // 4)[1].astype(F32), float(n), order)
    tri = lax.broadcasted_iota(jnp.int32, (TOK, TOK), 1) < lax.broadcasted_iota(jnp.int32, (TOK, TOK), 0)
    place = nn(jnp.where(tri, 1.0, 0.0).astype(BF16), hits.astype(BF16)) + order * PAD
    col = lax.broadcasted_iota(jnp.int32, (TOK, 32 * PAD), 1).astype(F32)
    w = jnp.zeros((TOK, 32 * PAD), F32)
    for k in range(TOP):
        at = jnp.sum(jnp.where(names[:, k : k + 1] == lane, place, 0.0), axis=1, keepdims=True)
        w = w + jnp.where(col == at, gw[:, k : k + 1], 0.0)
    for i in range(3):
        piece = w.astype(BF16)
        wmat[pl.ds(i * TOK, TOK), :] = piece
        w = w - piece.astype(F32)

    for q in (0, 1):
        y_copy(1, q).wait_recv()
        sib_copy(0, 1, q).start()
        x_copy(1, 0, q).wait_recv()
        sib_copy(0, 2, q).start()
        y_copy(0, q).wait_recv()
        sib_copy(0, 3, q).start()
        y_copy(2, q).start()
    x3_copy(0).start()
    for cp in weights:
        cp.wait()
    for q in (0, 1):
        for i in range(4):
            sib_copy(0, i, q).wait_recv()
    gather(0)
    stage_0(0)
    for q in (0, 1):
        y_copy(2, q).wait_recv()
    for dy in (2, 1, 3):
        for d in (0, 1):
            x_copy(d, dy).start()
    sib_copy(1, 1).start()
    stage(0, 1)

    def last_sum(g):
        for j in range(SRC):
            n = g * SRC + j
            pltpu.make_async_copy(rbuf.at[n], rbuf.at[n], rt_rs.at[n]).wait()
        rows = rbuf[pl.ds(g * SRC, SRC)].reshape(SRC * PAD, DC)
        parts = nn(wmat[:, pl.ds(g * SRC * PAD, SRC * PAD)], rows)
        parts = parts[2 * TOK :] + parts[TOK : 2 * TOK] + parts[:TOK]
        out_ref[...] = parts if g == 0 else out_ref[...] + parts

    def turn(i, _):
        factors = (i >= 1) & (i <= NG)

        @pl.when(i < NG)
        def _():
            stage(i, 2)

        @pl.when(i == NG + 1)
        def _():
            for g in range(NG - 1):
                last_sum(g)

        @pl.when(i >= 2)
        def _():
            last_stage(i - 2)

        @pl.when(i == 0)
        def _():
            for q in (0, 1):
                x_copy(0, 0, q).wait_recv()
            sib_copy(1, 0).start()
            x3_copy(0).wait_recv()
            sib_copy(1, 2).start()
            x_copy(0, 2).wait_recv()
            sib_copy(1, 3).start()
            x3_copy(2).start()
            for j in range(4):
                sib_copy(1, j).wait_recv()

        @pl.when(i == 1)
        def _():
            for dy in (1, 3, 2):
                x3_copy(dy).wait_recv()
                sib_copy(2, slot(2, dy)[1]).start()
            for j in range(4):
                sib_copy(2, j).wait_recv()

        @pl.when(i == 2)
        def _():
            for j in range(4):
                sib_copy(3, j).wait_recv()

        @pl.when(i < NG - 1)
        def _():
            gather(i + 1)
            stage_0(i + 1)

        @pl.when(factors)
        def _():
            gather_stage(i - 1, 1)

        @pl.when(i < NG)
        def _():
            stage(i, 3)

        @pl.when(factors)
        def _():
            gather_stage(i - 1, 2)

        @pl.when(i < NG - 1)
        def _():
            stage(i + 1, 1)

        @pl.when(i == 0)
        def _():
            x_copy(0, 3).wait_recv()
            x3_copy(3).start()
            x_copy(1, 1).wait_recv()
            x3_copy(1).start()
            x_copy(1, 2).wait_recv()
            sib_copy(2, 0).start()
            x_copy(1, 3).wait_recv()
            x_copy(0, 1).wait_recv()
            for j in range(4):
                sib_copy(3, j).start()

        @pl.when(i < NG)
        def _():
            stage_4(i)

        @pl.when(factors)
        def _():
            gather_stage(i - 1, 3)

        return 0

    lax.fori_loop(0, NG + 2, turn, 0)

    for q in (0, 1):
        for i in range(3):
            y_copy(i, q).wait_send()
        for d in (0, 1):
            x_copy(d, 0, q).wait_send()
        for i in range(4):
            sib_copy(0, i, q).wait_send()
    for i in range(4):
        x3_copy(i).wait_send()
        for g in range(1, NG):
            sib_copy(g, i).wait_send()
        for d in (0, 1):
            if i:
                x_copy(d, i).wait_send()

    def left(g, _):
        for d in (0, 1):
            for k in range(4):
                for h in (0, 1):
                    if k > 0 or h == d:

                        @pl.when(g >= 2)
                        def _():
                            rs_copy(g, d, k, h).wait_send()

                    if k < 3 or h == d:
                        for q in (0, 1):
                            ag_copy(g, d, k, h, q).wait_send()
        return 0

    lax.fori_loop(0, NG, left, 0)
    last_sum(NG - 1)

    for n in range(1, NG * SRC):
        back_copy(n // SRC, n % SRC).wait_send()


def shards(tokens, tangent, cotangent, routing, gate_weights, gate_proj, up_proj, down_proj):
    dma = pltpu.SemaphoreType.DMA
    anywhere = pl.BlockSpec(memory_space=pl.ANY)
    vmem = pl.BlockSpec(memory_space=pltpu.VMEM)
    return pl.pallas_call(
        kernel,
        out_shape=jax.ShapeDtypeStruct((TOK, DC), F32),
        in_specs=[anywhere] * 3 + [vmem] * 2 + [anywhere] * 3,
        out_specs=vmem,
        scratch_shapes=[
            pltpu.VMEM((DC, H), BF16),
            pltpu.VMEM((DC, H), BF16),
            pltpu.VMEM((H, DC), BF16),
            pltpu.VMEM((NG, 2, 4, BR, DC), BF16),
            pltpu.VMEM((2, 3 * GR, DC), BF16),
            pltpu.VMEM((5, SUMS * GR, CH), F32),
            pltpu.VMEM((32, MR, 128), jnp.int16),
            pltpu.VMEM((64, MR, 128), jnp.int16),
            pltpu.VMEM((NG * 16, 2 * GR, 128), BF16),
            pltpu.VMEM((GR, DC), F32),
            pltpu.VMEM((NG * SRC, PAD, DC), BF16),
            pltpu.VMEM((32, PAD, DC), BF16),
            pltpu.VMEM((3 * TOK, 32 * PAD), BF16),
            dma((3,)), dma((3,)), dma((6,)), dma((6,)), dma((10,)), dma((10,)), dma((4,)), dma((4,)),
            dma((20,)), dma((20,)), dma((32,)), dma((64,)), dma((128,)), dma((128,)), dma((32,)), dma((32,)),
        ],
        compiler_params=pltpu.CompilerParams(
            collective_id=0, has_side_effects=True, vmem_limit_bytes=61 * 1024 * 1024
        ),
        cost_estimate=pl.CostEstimate(
            flops=2 * 7 * 576 * DC * H, bytes_accessed=12_000_000, transcendentals=576 * H // NZ
        ),
    )(tokens, tangent, cotangent, routing.T, gate_weights.T, gate_proj[0], up_proj[0], down_proj[0])


def solution(mesh):
    in_specs = (
        P("expert", "dp"),
        P("expert", "dp"),
        P("expert", "dp"),
        P("expert", None),
        P("expert", None),
        P("expert", "dp", None),
        P("expert", "dp", None),
        P("expert", None, "dp"),
    )
    return jax.shard_map(
        shards, mesh=mesh, in_specs=in_specs, out_specs=P("expert", "dp"), check_vma=False
    )
```

time: 218 us -> 206 us (0.945)
  Pallas kernels: 212 us -> 203 us
  local copies, waits for them, and re-layouts: 4.4 us -> 1.64 us
    pallas_call x1, Pallas kernels: 212 us -> 203 us  [shards(): pl.pallas_call(kernel, out_shape=jax.ShapeDtypeStruct((TOK, DC), F32), in...]
    unnamed x3 -> x1, local copies, waits for them, and re-layouts: 4.4 us -> 1.64 us
where the time goes in v2:
time: 206 us; the launch traced here: 205 us
  Pallas kernels  203 us (99%)
    pallas_call x1, Pallas kernels, shards(): pl.pallas_call(kernel, out_shape=jax.ShapeDtypeStruct((TOK, DC), F32), in...  203 us

profile of v2, /device:TPU:1, one launch (start us, length us, event | category | flops | bytes accessed | tf_op | source)
XLA Modules:
  0.0 204.8 jit_solution(16128326374936633507)
XLA Ops:
  0.0 203.2 %shard_map.82 = f32[64,896]{1,0:T(8,128)} custom-call(bf16[64,896]{1,0:T(8,128)(2,1)} %x_ref.1, bf16[64,896]{1,0:T(8,128)(2,1)} %v_ref.1, bf16[64,896]{1,0:T(8,128)(2,1)} %c_ref.1, s32[8,64]{1,0:T(8,128)} %bitcast.8, f32[8,64]{1,0:T(8,128)} %bitcast.9, bf16[896,2048]{1,0:T(8,128)(2,1)} %bitcast.5, bf16[896,2048]{1,0:T(8,128)(2,1)} %bitcast.6, ...), custom_call_target="tpu_custom_call" | custom-call | flops 14797504512 | bytes 12000000 | tf_op jit(solution)/shard_map/pallas_call | solution.py:497
  203.2 1.6 copy.10

commit v3 on v2

--- a/solution.py
+++ b/solution.py
@@ -20,6 +20,7 @@
 SRC = 8
 GR = SRC * CAP
 SUMS = 5
+EARLY = 2
 CHIPS = (
     ((0, 0), (0, 1), (1, 0), (0, 3)),
     ((3, 0), (0, 2), (2, 0), (3, 2)),
@@ -29,6 +30,7 @@
 MR = SUMS * GR + 16
 BR = 16 + 3 * TOK
 PARTS = (pl.ds(0, 16 + TOK), pl.ds(16 + TOK, 2 * TOK))
+NEAR = 64
 PAD = 32
 
 
@@ -43,7 +45,7 @@
 def kernel(
     x_ref, v_ref, c_ref, routing_ref, gw_ref, gate_ref, up_ref, down_ref, out_ref,
     gate_v, up_v, down_v, tok, xrows, part, rs_s, rs_r, fac, acc, sbuf, rbuf, wmat,
-    w_sem, l_sem, y_ss, y_rs, x_ss, x_rs, x3_ss, x3_rs, sib_ss, sib_rs,
+    near_s, near_r, w_sem, l_sem, near_ss, near_rs, y_ss, y_rs, x_ss, x_rs, x3_ss, x3_rs, sib_ss, sib_rs,
     rs_ss, rs_rs, ag_ss, ag_rs, rt_ss, rt_rs,
 ):
     me = lax.axis_index("dp")
@@ -94,7 +96,6 @@
     twice = lax.broadcasted_iota(jnp.int32, (TOK, 128), 1) % TOK == lax.broadcasted_iota(jnp.int32, (TOK, 128), 0)
     tok[0, 0, 0, pl.ds(0, 16), :] = jnp.zeros((16, DC), BF16)
     tok[0, 0, 0, pl.ds(0, 16), pl.ds(0, 128)] = nn(named, jnp.where(twice, 1.0, 0.0).astype(BF16)).astype(BF16)
-    pl.semaphore_wait(bar, 33)
 
     def slot(col, dy):
         return next((g, i) for g in range(NG) for i in range(4) if CHIPS[g][i] == (col, dy))
@@ -105,26 +106,30 @@
             return tok.at[g, 0, i]
         return tok.at[g, 0, i, PARTS[q]]
 
-    def y_copy(i, q):
-        if i == 0:
-            return remote(block(0, 0, q), block(0, 3, q), y_ss.at[q], y_rs.at[q], y_dev[0])
-        if i == 1:
-            return remote(block(0, 0, q), block(0, 1, q), y_ss.at[2 + q], y_rs.at[2 + q], y_dev[1])
-        src = block(0, 3, q) if q == 0 else block(0, 1, q)
-        return remote(src, block(0, 2, q), y_ss.at[4 + q], y_rs.at[4 + q], y_dev[q])
-
-    def x_copy(d, dy, q=None):
-        i = d * 5 + (dy if dy else 4 * (q or 0))
-        return remote(block(0, dy, q), block(1 if d else 3, dy, q), x_ss.at[i], x_rs.at[i], x_dev[d])
+    def y_copy(i):
+        if i < 2:
+            return remote(block(0, 0), block(0, 1 if i else 3), y_ss.at[i], y_rs.at[i], y_dev[i])
+        q = i - 2
+        return remote(block(0, 1 if q else 3, q), block(0, 2, q), y_ss.at[i], y_rs.at[i], y_dev[q])
+
+    def x_copy(d, dy):
+        i = d * 4 + dy
+        return remote(block(0, dy), block(1 if d else 3, dy), x_ss.at[i], x_rs.at[i], x_dev[d])
 
     def x3_copy(dy):
         col, d = (1, 1) if dy < 2 else (3, 0)
         return remote(block(col, dy), block(2, dy), x3_ss.at[dy], x3_rs.at[dy], x_dev[d])
 
-    def sib_copy(g, i, q=None):
-        n = g * 4 + i + (16 if q == 1 else 0)
-        rows = pl.ds(0, BR) if q is None else PARTS[q]
-        return remote(tok.at[g, 0, i, rows], tok.at[g, 1, i, rows], sib_ss.at[n], sib_rs.at[n], sib_dev)
+    def sib_copy(g, i):
+        n = g * 4 + i
+        return remote(tok.at[g, 0, i], tok.at[g, 1, i], sib_ss.at[n], sib_rs.at[n], sib_dev)
+
+    def near_dev(j):
+        dx, dy = CHIPS[0][j % 4]
+        return at_xy(-dx, -dy, j // 4)
+
+    def near_copy(j):
+        return remote(near_s.at[j], near_r.at[j], near_ss.at[j], near_rs.at[j], near_dev(j))
 
     def rs_copy(g, d, k, h):
         s = (((g % 2) * 2 + d) * 4 + k) * 2 + h
@@ -170,6 +175,13 @@
             )
             xrows[g % 2, pl.ds(a * GR, GR), :] = nn(hot, rows).astype(BF16)
 
+    def gather_near():
+        r = lax.broadcasted_iota(jnp.int32, (3 * GR, SRC * NEAR), 0)
+        q = lax.broadcasted_iota(jnp.int32, (3 * GR, SRC * NEAR), 1)
+        from_ = (r % GR) // CAP * NEAR + r // GR * CAP + r % CAP
+        hot = jnp.where(q == from_, 1.0, 0.0).astype(BF16)
+        xrows[0] = nn(hot, jnp.concatenate([near_r[j] for j in range(SRC)], axis=0)).astype(BF16)
+
     def products(g, d, chunk):
         first = pl.multiple_of(chunk * CH, CH)
         cols = pl.ds(first, CH)
@@ -292,16 +304,36 @@
                     else:
                         back_copy(at, j).start()
 
-    loads[0].wait()
-    for q in (0, 1):
-        if q == 1:
-            loads[1].wait()
-            loads[2].wait()
-        y_copy(0, q).start()
-        y_copy(1, q).start()
-        x_copy(1, 0, q).start()
-        sib_copy(0, 0, q).start()
-        x_copy(0, 0, q).start()
+    thrice = lax.broadcasted_iota(jnp.int32, (TOK, 3 * TOK), 1) % TOK == lax.broadcasted_iota(jnp.int32, (TOK, 3 * TOK), 0)
+    wide = nn(named, jnp.where(thrice, 1.0, 0.0).astype(BF16))
+    at = lax.broadcasted_iota(jnp.int32, (SRC, 3 * TOK), 0)
+    hits = jnp.zeros((SRC, 3 * TOK), F32)
+    for j in range(SRC):
+        hit = jnp.sum(jnp.where(wide == near_dev(j)[1].astype(F32), 1.0, 0.0), axis=0, keepdims=True)
+        hits = jnp.where(at == j, hit, hits)
+    tri_r = lax.broadcasted_iota(jnp.int32, (3 * TOK, 3 * TOK), 0)
+    tri_c = lax.broadcasted_iota(jnp.int32, (3 * TOK, 3 * TOK), 1)
+    tri = jnp.where((tri_r < tri_c) & (tri_r // TOK == tri_c // TOK), 1.0, 0.0).astype(BF16)
+    first = (lax.broadcasted_iota(jnp.int32, (SRC, 3 * TOK), 1) // TOK * CAP).astype(F32)
+    target = jnp.where(hits > 0.5, nn(hits.astype(BF16), tri) + first, -1.0)
+    row = lax.broadcasted_iota(jnp.int32, (NEAR, 3 * TOK), 0).astype(F32)
+    hot = jnp.concatenate(
+        [jnp.where(row == target[j : j + 1], 1.0, 0.0).astype(BF16) for j in range(SRC)], axis=0
+    )
+    for cp in loads:
+        cp.wait()
+    near = nn(hot, tok[0, 0, 0, pl.ds(16, 3 * TOK), :]).astype(BF16)
+    for j in range(SRC):
+        near_s[j] = near[j * NEAR : (j + 1) * NEAR]
+    near_r[0] = near[0:NEAR]
+    pl.semaphore_wait(bar, 33)
+
+    for j in (1, 2, 3, 5, 6, 7, 4):
+        near_copy(j).start()
+    for i in (0, 1):
+        y_copy(i).start()
+    for d in (1, 0):
+        x_copy(d, 0).start()
 
     same = lax.broadcasted_iota(jnp.int32, (TOK, TOK), 0) == lax.broadcasted_iota(jnp.int32, (TOK, TOK), 1)
     same = jnp.where(same, 1.0, 0.0).astype(BF16)
@@ -332,29 +364,22 @@
         wmat[pl.ds(i * TOK, TOK), :] = piece
         w = w - piece.astype(F32)
 
-    for q in (0, 1):
-        y_copy(1, q).wait_recv()
-        sib_copy(0, 1, q).start()
-        x_copy(1, 0, q).wait_recv()
-        sib_copy(0, 2, q).start()
-        y_copy(0, q).wait_recv()
-        sib_copy(0, 3, q).start()
-        y_copy(2, q).start()
-    x3_copy(0).start()
     for cp in weights:
         cp.wait()
-    for q in (0, 1):
-        for i in range(4):
-            sib_copy(0, i, q).wait_recv()
-    gather(0)
+    for j in (4, 1, 2, 3, 5, 6, 7):
+        near_copy(j).wait_recv()
+    gather_near()
     stage_0(0)
-    for q in (0, 1):
-        y_copy(2, q).wait_recv()
-    for dy in (2, 1, 3):
-        for d in (0, 1):
-            x_copy(d, dy).start()
-    sib_copy(1, 1).start()
     stage(0, 1)
+    for i in (0, 1):
+        y_copy(i).wait_recv()
+        y_copy(2 + i).start()
+    for dy in (1, 3):
+        x_copy(0, dy).start()
+    x_copy(1, 0).wait_recv()
+    x3_copy(0).start()
+    for dy in (1, 3):
+        x_copy(1, dy).start()
 
     def last_sum(g):
         for j in range(SRC):
@@ -383,14 +408,18 @@
 
         @pl.when(i == 0)
         def _():
-            for q in (0, 1):
-                x_copy(0, 0, q).wait_recv()
-            sib_copy(1, 0).start()
+            y_copy(2).wait_recv()
+            y_copy(3).wait_recv()
+            for d in (0, 1):
+                x_copy(d, 2).start()
+            sib_copy(1, slot(0, 2)[1]).start()
+            stage(0, 3)
+            x_copy(0, 0).wait_recv()
+            sib_copy(1, slot(3, 0)[1]).start()
             x3_copy(0).wait_recv()
-            sib_copy(1, 2).start()
-            x_copy(0, 2).wait_recv()
-            sib_copy(1, 3).start()
-            x3_copy(2).start()
+            sib_copy(1, slot(2, 0)[1]).start()
+            x_copy(0, EARLY).wait_recv()
+            sib_copy(1, slot(3, EARLY)[1]).start()
             for j in range(4):
                 sib_copy(1, j).wait_recv()
 
@@ -416,7 +445,7 @@
         def _():
             gather_stage(i - 1, 1)
 
-        @pl.when(i < NG)
+        @pl.when((i > 0) & (i < NG))
         def _():
             stage(i, 3)
 
@@ -430,14 +459,16 @@
 
         @pl.when(i == 0)
         def _():
-            x_copy(0, 3).wait_recv()
+            for dy in (1, 3, 2):
+                if dy != EARLY:
+                    x_copy(0, dy).wait_recv()
             x3_copy(3).start()
-            x_copy(1, 1).wait_recv()
-            x3_copy(1).start()
-            x_copy(1, 2).wait_recv()
-            sib_copy(2, 0).start()
-            x_copy(1, 3).wait_recv()
-            x_copy(0, 1).wait_recv()
+            x3_copy(2).start()
+            for dy in (1, 3, 2):
+                x_copy(1, dy).wait_recv()
+                if dy == 1:
+                    x3_copy(1).start()
+            sib_copy(2, slot(1, 2)[1]).start()
             for j in range(4):
                 sib_copy(3, j).start()
 
@@ -453,20 +484,15 @@
 
     lax.fori_loop(0, NG + 2, turn, 0)
 
-    for q in (0, 1):
-        for i in range(3):
-            y_copy(i, q).wait_send()
-        for d in (0, 1):
-            x_copy(d, 0, q).wait_send()
-        for i in range(4):
-            sib_copy(0, i, q).wait_send()
+    for j in range(1, SRC):
+        near_copy(j).wait_send()
     for i in range(4):
+        y_copy(i).wait_send()
         x3_copy(i).wait_send()
         for g in range(1, NG):
             sib_copy(g, i).wait_send()
         for d in (0, 1):
-            if i:
-                x_copy(d, i).wait_send()
+            x_copy(d, i).wait_send()
 
     def left(g, _):
         for d in (0, 1):
@@ -513,8 +539,10 @@
             pltpu.VMEM((NG * SRC, PAD, DC), BF16),
             pltpu.VMEM((32, PAD, DC), BF16),
             pltpu.VMEM((3 * TOK, 32 * PAD), BF16),
-            dma((3,)), dma((3,)), dma((6,)), dma((6,)), dma((10,)), dma((10,)), dma((4,)), dma((4,)),
-            dma((20,)), dma((20,)), dma((32,)), dma((64,)), dma((128,)), dma((128,)), dma((32,)), dma((32,)),
+            pltpu.VMEM((SRC, NEAR, DC), BF16),
+            pltpu.VMEM((SRC, NEAR, DC), BF16),
+            dma((3,)), dma((3,)), dma((8,)), dma((8,)), dma((4,)), dma((4,)), dma((8,)), dma((8,)), dma((4,)), dma((4,)),
+            dma((16,)), dma((16,)), dma((32,)), dma((64,)), dma((128,)), dma((128,)), dma((32,)), dma((32,)),
         ],
         compiler_params=pltpu.CompilerParams(
             collective_id=0, has_side_effects=True, vmem_limit_bytes=61 * 1024 * 1024

time: 206 us -> 212 us (1.029)
  Pallas kernels: 203 us -> 211 us
    pallas_call x1, Pallas kernels: 203 us -> 211 us  [shards(): pl.pallas_call(kernel, out_shape=jax.ShapeDtypeStruct((TOK, DC), F32), in...]
where the time goes in v3:
time: 212 us
  Pallas kernels  211 us (100%)
    pallas_call x1, Pallas kernels, shards(): pl.pallas_call(kernel, out_shape=jax.ShapeDtypeStruct((TOK, DC), F32), in...  211 us

profile of v3, /device:TPU:1, one launch (start us, length us, event | category | flops | bytes accessed | tf_op | source)
XLA Modules:
  0.0 212.2 jit_solution(7355532022178669634)
XLA Ops:
  0.0 210.6 %shard_map.82 = f32[64,896]{1,0:T(8,128)} custom-call(bf16[64,896]{1,0:T(8,128)(2,1)} %x_ref.1, bf16[64,896]{1,0:T(8,128)(2,1)} %v_ref.1, bf16[64,896]{1,0:T(8,128)(2,1)} %c_ref.1, s32[8,64]{1,0:T(8,128)} %bitcast.8, f32[8,64]{1,0:T(8,128)} %bitcast.9, bf16[896,2048]{1,0:T(8,128)(2,1)} %bitcast.5, bf16[896,2048]{1,0:T(8,128)(2,1)} %bitcast.6, ...), custom_call_target="tpu_custom_call" | custom-call | flops 14797504512 | bytes 12000000 | tf_op jit(solution)/shard_map/pallas_call | solution.py:523
  210.6 1.6 copy.10

commit v4 on v3

--- a/solution.py
+++ b/solution.py
@@ -374,8 +374,6 @@
     for i in (0, 1):
         y_copy(i).wait_recv()
         y_copy(2 + i).start()
-    for dy in (1, 3):
-        x_copy(0, dy).start()
     x_copy(1, 0).wait_recv()
     x3_copy(0).start()
     for dy in (1, 3):
@@ -412,6 +410,8 @@
             y_copy(3).wait_recv()
             for d in (0, 1):
                 x_copy(d, 2).start()
+            for dy in (1, 3):
+                x_copy(0, dy).start()
             sib_copy(1, slot(0, 2)[1]).start()
             stage(0, 3)
             x_copy(0, 0).wait_recv()

time: 212 us -> 211 us (level)
  no operation moved by 1% of the time
where the time goes in v4:
time: 211 us
  Pallas kernels  210 us (100%)
    pallas_call x1, Pallas kernels, shards(): pl.pallas_call(kernel, out_shape=jax.ShapeDtypeStruct((TOK, DC), F32), in...  210 us

profile of v4, /device:TPU:1, one launch (start us, length us, event | category | flops | bytes accessed | tf_op | source)
XLA Modules:
  0.0 211.3 jit_solution(7416720195120982982)
XLA Ops:
  0.0 209.6 %shard_map.82 = f32[64,896]{1,0:T(8,128)} custom-call(bf16[64,896]{1,0:T(8,128)(2,1)} %x_ref.1, bf16[64,896]{1,0:T(8,128)(2,1)} %v_ref.1, bf16[64,896]{1,0:T(8,128)(2,1)} %c_ref.1, s32[8,64]{1,0:T(8,128)} %bitcast.8, f32[8,64]{1,0:T(8,128)} %bitcast.9, bf16[896,2048]{1,0:T(8,128)(2,1)} %bitcast.5, bf16[896,2048]{1,0:T(8,128)(2,1)} %bitcast.6, ...), custom_call_target="tpu_custom_call" | custom-call | flops 14797504512 | bytes 12000000 | tf_op jit(solution)/shard_map/pallas_call | solution.py:523
  209.7 1.6 copy.10

commit v5 on v2

--- a/solution.py
+++ b/solution.py
@@ -383,6 +383,7 @@
 
         @pl.when(i == 0)
         def _():
+            stage(0, 3)
             for q in (0, 1):
                 x_copy(0, 0, q).wait_recv()
             sib_copy(1, 0).start()
@@ -416,7 +417,7 @@
         def _():
             gather_stage(i - 1, 1)
 
-        @pl.when(i < NG)
+        @pl.when((i > 0) & (i < NG))
         def _():
             stage(i, 3)
 

time: 206 us -> 206 us (level)
  no operation moved by 1% of the time
where the time goes in v5:
time: 206 us; the launch traced here: 205 us
  Pallas kernels  203 us (99%)
    pallas_call x1, Pallas kernels, shards(): pl.pallas_call(kernel, out_shape=jax.ShapeDtypeStruct((TOK, DC), F32), in...  203 us

profile of v5, /device:TPU:1, one launch (start us, length us, event | category | flops | bytes accessed | tf_op | source)
XLA Modules:
  0.0 204.8 jit_solution(14705835694876610761)
XLA Ops:
  0.0 203.1 %shard_map.82 = f32[64,896]{1,0:T(8,128)} custom-call(bf16[64,896]{1,0:T(8,128)(2,1)} %x_ref.1, bf16[64,896]{1,0:T(8,128)(2,1)} %v_ref.1, bf16[64,896]{1,0:T(8,128)(2,1)} %c_ref.1, s32[8,64]{1,0:T(8,128)} %bitcast.8, f32[8,64]{1,0:T(8,128)} %bitcast.9, bf16[896,2048]{1,0:T(8,128)(2,1)} %bitcast.5, bf16[896,2048]{1,0:T(8,128)(2,1)} %bitcast.6, ...), custom_call_target="tpu_custom_call" | custom-call | flops 14797504512 | bytes 12000000 | tf_op jit(solution)/shard_map/pallas_call | solution.py:498
  203.1 1.6 copy.10
